TPU v7x, 256 devices: a whole 4x4x8 slice. The times are simulated.
256 devices in a mesh: lat: 32 (over y, z_lo, core), lev: 8 (over x, z_hi).
Axes of the slice: x: 4, y: 4, z: 8 (z_hi: 2, z_lo: 4; z = z_hi * 4 + z_lo), core: 2. Of those that a mesh axis runs over, the one named last changes fastest.
Arguments:
- increment: float32 [2, 16, 128, 2048], P(None, 'lev', 'lat'), may hold values from -6 to 6
- deviations: float32 [2, 16, 128, 2048], P(None, 'lev', 'lat'), may hold values from 3 to 12
- diffuse_x: float32 [16, 128, 2048], P('lev', 'lat'), may hold values from 1000 to 4000
- diffuse_y: float32 [16, 128, 2048], P('lev', 'lat'), may hold values from 256 to 640
- diffuse_z: float32 [16, 128, 2048], P('lev', 'lat'), may hold values from 4 to 64
- sea_mask: int32 [16, 128, 2048], P('lev', 'lat'), may hold values from 0 to 1, as said below
Outputs:
- covariance_out: float32 [2, 16, 128, 2048], P(None, 'lev', 'lat')
Inputs may be any that keep to these rules, and one draw needn't show every extreme that they name: `sea_mask`: A cell that is land at one level is land at every deeper level.
All inputs are finite; a program needn't handle non-finite values.
Results may differ from a plain program's by a relative error of at most 0.0003.
Values sent between devices are 32-bit elements; how exact they have to be, the bound alone decides.
A program may use at most 64 MiB of HBM per device.

v0:
```python
import math

import jax
import jax.numpy as jnp
from jax import lax
from jax.experimental import pallas as pl
from jax.experimental.pallas import tpu as pltpu
from jax.sharding import PartitionSpec as P

MESH = pl.DeviceIdType.MESH
F32 = jnp.float32
LEVELS, HALF, TILES, BLOCK, ROWS = 16, 1024, 8, 16, 128
STRIDES = (1, 2, 4, 8, 16, 32, 64, 128, 256, 512, 1024)
TO_COLUMNS, TO_LINES, COUPLINGS, NEXT_ROW, REDUCED, LATITUDE, BACK_COLUMNS, BACK_ROWS = 0, 1, 2, 3, 4, 5, 9, 10


def swap_halves(tile):
    return pltpu.roll(tile, 4, 0)


def from_west(tiles, stride, lane):
    if stride >= 128:
        k = stride // 128
        return [tiles[j - k] if j >= k else swap_halves(tiles[TILES + j - k]) for j in range(TILES)]
    turned = [pltpu.roll(tile, stride, 1) for tile in tiles]
    carry = [swap_halves(turned[-1])] + turned[:-1]
    return [jnp.where(lane < stride, c, t) for c, t in zip(carry, turned)]


def from_east(tiles, stride, lane):
    if stride >= 128:
        k = stride // 128
        return [tiles[j + k] if j + k < TILES else swap_halves(tiles[j + k - TILES]) for j in range(TILES)]
    turned = [pltpu.roll(tile, 128 - stride, 1) for tile in tiles]
    carry = turned[1:] + [swap_halves(turned[0])]
    return [jnp.where(lane >= 128 - stride, c, t) for c, t in zip(carry, turned)]


def paired(rows):
    return jnp.concatenate([rows[:, :HALF], rows[:, HALF:]], axis=0)


def tiles_of(wide):
    return [wide[:, 128 * j : 128 * (j + 1)] for j in range(TILES)]


def kernel(
    inc_hbm, dev_hbm, dx_hbm, dy_hbm, dz_hbm, sea_hbm, out_ref,
    inc, dev, dx, dy, dz, mask, scale,
    z_send, z_recv, z_factor, z_out, g_recv, c_send, c_recv, n_send, n_recv,
    x_factor, x_last, y_factor, r_all, inverse, y_all, grid, zb_recv, zb_out, r_recv,
    in_sem, send_sem, recv_sem,
):
    lat, lev = lax.axis_index("lat"), lax.axis_index("lev")
    y, zl, core = lat // 8, (lat // 2) % 4, lat % 2
    x, zh = lev // 2, lev % 2
    mine = y * 2 + core
    lane = lax.broadcasted_iota(jnp.int32, (8, 128), 1)
    sublane = lax.broadcasted_iota(jnp.int32, (8, 128), 0)

    def at(y_, zl_, core_, x_, zh_):
        return {"lat": y_ * 8 + zl_ * 2 + core_, "lev": x_ * 2 + zh_}

    def send(src, dst, phase, target):
        pltpu.make_async_remote_copy(
            src_ref=src, dst_ref=dst, send_sem=send_sem.at[phase], recv_sem=recv_sem.at[phase],
            device_id=target, device_id_type=MESH,
        ).start()

    def send_or_keep(src, dst, phase, target, here):
        @pl.when(here)
        def _():
            pltpu.make_async_copy(src, dst, recv_sem.at[phase]).start()

        @pl.when(jnp.logical_not(here))
        def _():
            send(src, dst, phase, target)

    def wait(ref, sem):
        pltpu.make_async_copy(ref, ref, sem).wait()

    loads = [
        pltpu.make_async_copy(src, dst, in_sem.at[i])
        for i, (src, dst) in enumerate(
            [(sea_hbm, mask), (dev_hbm, dev), (inc_hbm, inc), (dz_hbm, dz), (dx_hbm, dx), (dy_hbm, dy)]
        )
    ]
    for load in loads:
        load.start()

    zf = (zl + 2) % 4
    greeted = [at(y, zf, core, (x + a) % 4, (zh + b) % 2) for a in (2, 1, 3, 0) for b in (0, 1)]
    greeted += [
        at(y, (zl + a) % 4, (core + d) % 2, x, (zh + b) % 2)
        for a in range(4) for b in range(2) for d in range(2)
        if (a, b, d) != (0, 0, 0) and (a, d) != (2, 0)
    ]
    greeted += [at((y + a) % 4, zl, d, x, zh) for a in (2, 1, 3) for d in range(2)]
    barrier = pltpu.get_barrier_semaphore()
    for target in greeted:
        pl.semaphore_signal(barrier, inc=1, device_id=target, device_id_type=MESH)

    for load in loads[:4]:
        load.wait()
    sea = [paired(mask[l]).astype(F32) for l in range(2)]
    for l in range(2):
        couple = tiles_of(paired(dz[l]) * sea[l])
        for t in range(2):
            factor = paired(dev[t, l]) * sea[l]
            state = tiles_of(factor * paired(inc[t, l]))
            factor = tiles_of(factor)
            for j in range(TILES):
                scale[t, l, 8 * j : 8 * j + 8, :] = factor[j]
                spot = pl.ds(8 * (j % 2), 8)
                z_send[t, j // 2, 0, l, spot, :] = state[j]
                z_send[t, j // 2, 1, l, spot, :] = couple[j]
    for load in loads[4:]:
        load.wait()
    for l in range(2):
        sea_tiles = tiles_of(sea[l])
        west = from_west(sea_tiles, 1, lane)
        west[0] = jnp.where((lane == 0) & (sublane < 4), 0.0, west[0])
        couple_x, couple_y = tiles_of(paired(dx[l])), tiles_of(paired(dy[l]))
        for j in range(TILES):
            c_send[l, 0, 8 * j : 8 * j + 8, :] = couple_x[j] * sea_tiles[j] * west[j]
            c_send[l, 1, 8 * j : 8 * j + 8, :] = couple_y[j] * sea_tiles[j]

    pl.semaphore_wait(barrier, len(greeted))

    for a in (2, 1, 3, 0):
        j = (x + a) % 4
        for t in range(2):
            send(z_send.at[t, j], z_recv.at[lev], TO_COLUMNS, at(y, zf, core, j, t))
    part = (zl % 2) * 2 + core
    lines_core = zl // 2
    for l in range(2):
        zt = 2 * zh + l
        for b in (1, 0):
            target = at(y, zt, lines_core, x, (zh + b) % 2)
            src, dst = c_send.at[l], c_recv.at[:, pl.ds(pl.multiple_of(part * 64, 64), 64)]
            if b == 0:
                send_or_keep(src, dst, COUPLINGS, target, (zl == zt) & (core == lines_core))
            else:
                send(src, dst, COUPLINGS, target)

    def solve_levels(take, put):
        upper, lower = take(0), take(15)
        held = {0: upper, 15: lower}
        for k in range(7):
            held[k + 1] = take(k + 1) + z_factor[0, k] * held[k]
            held[14 - k] = take(14 - k) + z_factor[0, 15 - k] * held[15 - k]
        solved = z_factor[1, 8] * (held[8] + z_factor[0, 7] * held[7])
        put(8, solved)
        up = down = solved
        for k in range(8):
            up = z_factor[1, 7 - k] * held[7 - k] + z_factor[0, 7 - k] * up
            put(7 - k, up)
            if k < 7:
                down = z_factor[1, 9 + k] * held[9 + k] + z_factor[0, 9 + k] * down
                put(9 + k, down)

    wait(z_recv, recv_sem.at[TO_COLUMNS])
    upper = lower = jnp.ones((16, 128), F32)
    for k in range(8):
        c_up = z_recv[(k + 1) // 2, 1, (k + 1) % 2]
        inv = 1.0 / (upper + c_up)
        z_factor[0, k] = c_up * inv
        z_factor[1, k] = inv
        upper = 1.0 + c_up * inv * upper
        if k < 7:
            c_low = z_recv[(15 - k) // 2, 1, (15 - k) % 2]
            inv = 1.0 / (lower + c_low)
            z_factor[0, 15 - k] = c_low * inv
            z_factor[1, 15 - k] = inv
            lower = 1.0 + c_low * inv * lower
    z_factor[1, 8] = 1.0 / (upper + (lower - 1.0))

    def put_first(k, value):
        z_out[k] = value

    solve_levels(lambda k: z_recv[k // 2, 0, k % 2], put_first)

    from_core = zf // 2
    from_part = (zf % 2) * 2 + core
    for a in (2, 1, 3, 0):
        for b in (3, 1, 2, 0):
            x_, zl_ = (x + a) % 4, (zl + b) % 4
            src = z_out.at[x_ * 4 + zl_]
            dst = g_recv.at[pl.ds(pl.multiple_of(from_part * 64 + x * 16, 16), 16)]
            target = at(y, zl_, from_core, x_, zh)
            if a == 0 and b == 0:
                send_or_keep(src, dst, TO_LINES, target, from_core == core)
            else:
                send(src, dst, TO_LINES, target)

    wait(c_recv, recv_sem.at[COUPLINGS])

    def row_at(i, half):
        return pl.ds((i // 4) * 64 + (i % 4) + 32 * half, 8, stride=4)

    for half in range(2):
        n_send[8 * half : 8 * half + 8, :] = c_recv[1, row_at(0, half), :]
    before = (mine + 7) % 8
    send(n_send, n_recv, NEXT_ROW, at(before // 2, zl, before % 2, x, zh))

    def longitude_factor(part_, carry):
        base = pl.multiple_of(part_ * 64, 64)
        k = [c_recv[0, pl.ds(base + 8 * j, 8), :] for j in range(TILES)]
        e = [jnp.ones((8, 128), F32)] * TILES
        for i, stride in enumerate(STRIDES):
            k_east = from_east(k, stride, lane)
            inv = [1.0 / (a + (b + c)) for a, b, c in zip(e, k, k_east)]
            plus = [a * b for a, b in zip(k_east, inv)]
            minus = [a * b for a, b in zip(k, inv)]
            for j in range(TILES):
                x_factor[i, 0, pl.ds(base + 8 * j, 8), :] = plus[j]
                x_factor[i, 1, pl.ds(base + 8 * j, 8), :] = minus[j]
            west = from_west([a * b for a, b in zip(plus, e)], stride, lane)
            east = from_east([a * b for a, b in zip(minus, e)], stride, lane)
            k = from_west([a * b for a, b in zip(plus, k)], stride, lane)
            e = [a + (b + c) for a, b, c in zip(e, west, east)]
        for j in range(TILES):
            x_last[pl.ds(base + 8 * j, 8), :] = 1.0 / e[j]
        return carry

    lax.fori_loop(0, 4, longitude_factor, 0)

    wait(n_recv, recv_sem.at[NEXT_ROW])
    for half in range(2):
        spot = pl.ds(8 * half, 8)
        faces = [c_recv[1, row_at(i, half), :] for i in range(BLOCK)]
        north = jnp.where(mine < 7, n_recv[spot, :], 0.0)
        couple = [None] + [
            jnp.where(faces[i - 1] > 0.0, faces[i] if i < BLOCK else north, 0.0) for i in range(1, BLOCK + 1)
        ]
        ground = jnp.ones((8, 128), F32)
        own, link = jnp.ones((8, 128), F32), couple[1]
        to_own, to_next = [None] * BLOCK, [None] * BLOCK
        for i in range(1, BLOCK):
            inv = 1.0 / (ground + (link + couple[i + 1]))
            to_own[i], to_next[i] = link * inv, couple[i + 1] * inv
            y_factor[0, i, spot, :] = to_own[i]
            y_factor[1, i, spot, :] = to_next[i]
            y_factor[2, i, spot, :] = inv
            own = own + to_own[i] * ground
            link = to_own[i] * couple[i + 1]
            beyond = to_next[i] * ground
            ground = 1.0 + beyond
        r_all[mine, 0, spot, :] = own
        r_all[mine, 1, spot, :] = beyond
        r_all[mine, 2, spot, :] = link
        left, right = to_own[15], to_next[15]
        y_factor[3, 15, spot, :] = left
        y_factor[4, 15, spot, :] = right
        for i in range(BLOCK - 2, 0, -1):
            left = to_own[i] + to_next[i] * left
            right = to_next[i] * right
            y_factor[3, i, spot, :] = left
            y_factor[4, i, spot, :] = right

    ring = []
    for k in (4, 5, 3, 2, 6, 7, 1):
        block = (mine + k) % 8
        ring.append(at(block // 2, zl, block % 2, x, zh))
    for target in ring:
        send(r_all.at[mine], r_all.at[mine], REDUCED, target)

    def longitude_solve(source):
        def one(part_, carry):
            base = pl.multiple_of(part_ * 64, 64)
            r = [source[pl.ds(base + 8 * j, 8), :] for j in range(TILES)]
            for i, stride in enumerate(STRIDES):
                west = from_west([x_factor[i, 0, pl.ds(base + 8 * j, 8), :] * r[j] for j in range(TILES)], stride, lane)
                east = from_east([x_factor[i, 1, pl.ds(base + 8 * j, 8), :] * r[j] for j in range(TILES)], stride, lane)
                r = [a + (b + c) for a, b, c in zip(r, west, east)]
            for j in range(TILES):
                grid[pl.ds(base + 8 * j, 8), :] = r[j] * x_last[pl.ds(base + 8 * j, 8), :]
            return carry

        lax.fori_loop(0, 4, one, 0)

    def reduced_inverse():
        for half in range(2):
            spot = pl.ds(8 * half, 8)
            ground = [r_all[b, 0, spot, :] for b in range(8)]
            for b in range(1, 8):
                ground[b] = ground[b] + r_all[b - 1, 1, spot, :]
            link = [r_all[b, 2, spot, :] for b in range(7)]
            below, above = [ground[0]], [None] * 7 + [jnp.zeros((8, 128), F32)]
            north, south = [None] * 8, [None] * 8
            for b in range(7):
                north[b] = link[b] / (below[b] + link[b])
                below.append(ground[b + 1] + north[b] * below[b])
            for b in range(7, 0, -1):
                total = ground[b] + above[b]
                south[b] = link[b - 1] / (total + link[b - 1])
                above[b - 1] = south[b] * total
            for which in range(2):
                spike = mine + which
                row = [None] * 8
                here = jnp.zeros((8, 128), F32)
                for b in range(7, -1, -1):
                    moved = here if b == 7 else north[b] * here
                    here = jnp.where(spike == b, 1.0 / (below[b] + above[b]), moved)
                    row[b] = here
                here = jnp.zeros((8, 128), F32)
                for b in range(8):
                    moved = here if b == 0 else south[b] * here
                    here = jnp.where(spike < b, moved, row[b])
                    inverse[which, b, spot, :] = here

    def latitude_solve(rows, step, between=None):
        held = []
        for half in range(2):
            spot = pl.ds(8 * half, 8)
            own, here = rows(0, half), rows(1, half)
            mid = [None]
            for i in range(1, BLOCK):
                mid.append(y_factor[2, i, spot, :] * here)
                own = own + y_factor[0, i, spot, :] * here
                here = y_factor[1, i, spot, :] * here
                if i + 1 < BLOCK:
                    here = rows(i + 1, half) + here
            y_all[step, mine, spot, :] = own
            y_all[step, mine, pl.ds(16 + 8 * half, 8), :] = here
            held.append(mid)
        for target in ring:
            send(y_all.at[step, mine], y_all.at[step, mine], LATITUDE + step, target)
        for half in range(2):
            spot = pl.ds(8 * half, 8)
            for i in range(BLOCK - 2, 0, -1):
                held[half][i] = held[half][i] + y_factor[1, i, spot, :] * held[half][i + 1]
        if between is not None:
            between()
        wait(y_all.at[step, pl.ds(0, 7)], recv_sem.at[LATITUDE + step])
        result = []
        for half in range(2):
            spot = pl.ds(8 * half, 8)
            ends = []
            right = []
            for b in range(8):
                value = y_all[step, b, spot, :]
                if b > 0:
                    value = value + y_all[step, b - 1, pl.ds(16 + 8 * half, 8), :]
                right.append(value)
            for which in range(2):
                terms = [inverse[which, b, spot, :] * right[b] for b in range(8)]
                while len(terms) > 1:
                    terms = [a + b for a, b in zip(terms[::2], terms[1::2])]
                ends.append(terms[0])
            result.append(
                [ends[0]]
                + [
                    held[half][i] + (y_factor[3, i, spot, :] * ends[0] + y_factor[4, i, spot, :] * ends[1])
                    for i in range(1, BLOCK)
                ]
            )
        return result

    def from_grid(i, half):
        return grid[row_at(i, half), :]

    def to_grid(result):
        for half in range(2):
            for i in range(BLOCK):
                grid[row_at(i, half), :] = result[half][i]

    def first_between():
        wait(r_all.at[pl.ds(0, 7)], recv_sem.at[REDUCED])
        reduced_inverse()

    row = (mine * BLOCK + lax.broadcasted_iota(jnp.int32, (BLOCK, 128), 0)).astype(F32)
    weight = jnp.cos((-78.0 + 166.0 * (row + 0.5) / ROWS) * (math.pi / 180.0))

    wait(g_recv, recv_sem.at[TO_LINES])
    longitude_solve(g_recv)
    to_grid(latitude_solve(from_grid, 0, first_between))
    longitude_solve(grid)
    forward = latitude_solve(from_grid, 1)
    weighted = [[forward[half][i] * weight[i : i + 1, :] for i in range(BLOCK)] for half in range(2)]
    to_grid(latitude_solve(lambda i, half: weighted[half][i], 2))
    longitude_solve(grid)
    to_grid(latitude_solve(from_grid, 3))
    longitude_solve(grid)

    level = x * 4 + zl
    for a in (2, 1, 3, 0):
        x_ = (x + a) % 4
        for b in range(4):
            zl_, core_ = (2 * core + b // 2 + 2) % 4, b % 2
            src = grid.at[pl.ds(pl.multiple_of(b * 64 + x_ * 16, 16), 16)]
            target = at(y, zl_, core_, x_, zh)
            if a == 0:
                send_or_keep(src, zb_recv.at[level], BACK_COLUMNS, target, (zl_ == zl) & (core_ == core))
            else:
                send(src, zb_recv.at[level], BACK_COLUMNS, target)
    wait(zb_recv, recv_sem.at[BACK_COLUMNS])

    def put_last(k, value):
        zb_out[k] = value

    solve_levels(lambda k: zb_recv[k], put_last)
    for a in (2, 1, 3, 0):
        for b in range(2):
            x_ = (x + a) % 4
            src = zb_out.at[pl.ds(x_ * 4 + b * 2, 2)]
            dst = r_recv.at[zh, :, pl.ds(pl.multiple_of(x * 16, 16), 16)]
            send(src, dst, BACK_ROWS, at(y, zf, core, x_, b))
    wait(r_recv, recv_sem.at[BACK_ROWS])
    for t in range(2):
        for l in range(2):
            for j in range(TILES):
                spot = pl.ds(8 * j, 8)
                tile = scale[t, l, spot, :] * r_recv[t, l, spot, :]
                out_ref[t, l, :, 128 * j : 128 * j + 128] = tile[:4]
                out_ref[t, l, :, HALF + 128 * j : HALF + 128 * j + 128] = tile[4:]

    wait(z_send.at[:, :, :, :], send_sem.at[TO_COLUMNS])
    for l in range(2):
        wait(c_send.at[l], send_sem.at[COUPLINGS])
        kept = (zl == 2 * zh + l) & (core == lines_core)

        @pl.when(jnp.logical_not(kept))
        def _():
            wait(c_send.at[l], send_sem.at[COUPLINGS])

    wait(z_out.at[pl.ds(0, 15)], send_sem.at[TO_LINES])

    @pl.when(from_core != core)
    def _():
        wait(z_out.at[15], send_sem.at[TO_LINES])

    wait(n_send, send_sem.at[NEXT_ROW])
    wait(r_all.at[pl.ds(0, 7)], send_sem.at[REDUCED])
    for step in range(4):
        wait(y_all.at[step, pl.ds(0, 7)], send_sem.at[LATITUDE + step])
    wait(zb_recv.at[pl.ds(0, 15)], send_sem.at[BACK_COLUMNS])
    base = (zl - 2 * core + 2) % 4

    @pl.when(base >= 2)
    def _():
        wait(zb_recv.at[15], send_sem.at[BACK_COLUMNS])

    wait(r_recv, send_sem.at[BACK_ROWS])


def per_device(increment, deviations, diffuse_x, diffuse_y, diffuse_z, sea_mask):
    vmem = lambda *shape: pltpu.VMEM(shape, F32)
    shape = increment.shape
    plane = diffuse_x.shape
    return pl.pallas_call(
        kernel,
        out_shape=jax.ShapeDtypeStruct(shape, F32),
        in_specs=[pl.BlockSpec(memory_space=pl.ANY)] * 6,
        out_specs=pl.BlockSpec(memory_space=pltpu.VMEM),
        scratch_shapes=[
            vmem(*shape), vmem(*shape), vmem(*plane), vmem(*plane), vmem(*plane), pltpu.VMEM(plane, jnp.int32),
            vmem(2, 2, 64, 128),
            vmem(2, 4, 2, 2, 16, 128), vmem(8, 2, 2, 16, 128), vmem(2, 16, 16, 128), vmem(16, 16, 128),
            vmem(256, 128), vmem(2, 2, 64, 128), vmem(2, 256, 128), vmem(16, 128), vmem(16, 128),
            vmem(11, 2, 256, 128), vmem(256, 128), vmem(5, 16, 16, 128), vmem(8, 3, 16, 128), vmem(2, 8, 16, 128),
            vmem(4, 8, 32, 128), vmem(256, 128), vmem(16, 16, 128), vmem(16, 16, 128), vmem(2, 2, 64, 128),
            pltpu.SemaphoreType.DMA((6,)), pltpu.SemaphoreType.DMA((11,)), pltpu.SemaphoreType.DMA((11,)),
        ],
        compiler_params=pltpu.CompilerParams(
            collective_id=0, has_side_effects=True, vmem_limit_bytes=32 * 1024 * 1024
        ),
        name="covariance",
    )(increment, deviations, diffuse_x, diffuse_y, diffuse_z, sea_mask)


def solution(mesh):
    in_specs = (
        P(None, "lev", "lat", None),
        P(None, "lev", "lat", None),
        P("lev", "lat", None),
        P("lev", "lat", None),
        P("lev", "lat", None),
        P("lev", "lat", None),
    )
    out_specs = P(None, "lev", "lat", None)
    return jax.shard_map(
        per_device, mesh=mesh, in_specs=in_specs, out_specs=out_specs, check_vma=False
    )
```

profile of v0, /device:TPU:32, one launch (start us, length us, event | category | flops | bytes accessed | tf_op | source)
XLA Modules:
  0.0 75.1 jit_solution(14665433925146384763)
XLA Ops:
  0.0 0.0 copy-start
  0.0 0.9 %copy-done = f32[2,2,4,2048]{3,2,1,0:T(4,128)S(1)} copy-done((f32[2,2,4,2048]{3,2,1,0:T(4,128)S(1)}, f32[2,2,4,2048]{3,2,1,0:T(4,128)}, u32[]{:S(2)}) %copy-start) | copy-done | bytes 131096
  0.9 0.0 copy-start.1
  0.9 0.9 %copy-done.1 = f32[2,2,4,2048]{3,2,1,0:T(4,128)S(1)} copy-done((f32[2,2,4,2048]{3,2,1,0:T(4,128)S(1)}, f32[2,2,4,2048]{3,2,1,0:T(4,128)}, u32[]{:S(2)}) %copy-start.1) | copy-done | bytes 131096
  1.8 0.0 copy-start.2
  1.8 0.8 %copy-done.2 = f32[2,4,2048]{2,1,0:T(4,128)S(1)} copy-done((f32[2,4,2048]{2,1,0:T(4,128)S(1)}, f32[2,4,2048]{2,1,0:T(4,128)}, u32[]{:S(2)}) %copy-start.2) | copy-done | bytes 65560
  2.6 0.0 copy-start.3
  2.7 0.8 %copy-done.3 = f32[2,4,2048]{2,1,0:T(4,128)S(1)} copy-done((f32[2,4,2048]{2,1,0:T(4,128)S(1)}, f32[2,4,2048]{2,1,0:T(4,128)}, u32[]{:S(2)}) %copy-start.3) | copy-done | bytes 65560
  3.5 0.0 copy-start.4
  3.5 0.8 %copy-done.4 = f32[2,4,2048]{2,1,0:T(4,128)S(1)} copy-done((f32[2,4,2048]{2,1,0:T(4,128)S(1)}, f32[2,4,2048]{2,1,0:T(4,128)}, u32[]{:S(2)}) %copy-start.4) | copy-done | bytes 65560
  4.3 0.0 copy-start.5
  4.3 0.8 %copy-done.5 = s32[2,4,2048]{2,1,0:T(4,128)S(1)} copy-done((s32[2,4,2048]{2,1,0:T(4,128)S(1)}, s32[2,4,2048]{2,1,0:T(4,128)}, u32[]{:S(2)}) %copy-start.5) | copy-done | bytes 65560
  5.2 69.2 %covariance.1 = f32[2,2,4,2048]{3,2,1,0:T(4,128)S(1)} custom-call(f32[2,2,4,2048]{3,2,1,0:T(4,128)S(1)} %copy-done, f32[2,2,4,2048]{3,2,1,0:T(4,128)S(1)} %copy-done.1, f32[2,4,2048]{2,1,0:T(4,128)S(1)} %copy-done.2, f32[2,4,2048]{2,1,0:T(4,128)S(1)} %copy-done.3, f32[2,4,2048]{2,1,0:T(4,128)S(1)} %copy-done.4, s32[2,4,2048]{2,1,0:T(4,128)S(1)} %copy-done.5), custom_call_target="tpu_custom_call" | custom-call | tf_op jit(solution)/shard_map/covariance/pallas_call | solution.py:451
  74.4 0.7 copy.8
Async XLA Ops:
  0.0 0.9 %copy-start = (f32[2,2,4,2048]{3,2,1,0:T(4,128)S(1)}, f32[2,2,4,2048]{3,2,1,0:T(4,128)}, u32[]{:S(2)}) copy-start(f32[2,2,4,2048]{3,2,1,0:T(4,128)} %inc_hbm.1) | copy-start | bytes 393220
  0.9 0.9 %copy-start.1 = (f32[2,2,4,2048]{3,2,1,0:T(4,128)S(1)}, f32[2,2,4,2048]{3,2,1,0:T(4,128)}, u32[]{:S(2)}) copy-start(f32[2,2,4,2048]{3,2,1,0:T(4,128)} %dev_hbm.1) | copy-start | bytes 393220
  1.8 0.8 %copy-start.2 = (f32[2,4,2048]{2,1,0:T(4,128)S(1)}, f32[2,4,2048]{2,1,0:T(4,128)}, u32[]{:S(2)}) copy-start(f32[2,4,2048]{2,1,0:T(4,128)} %dx_hbm.1) | copy-start | bytes 196612
  2.6 0.8 %copy-start.3 = (f32[2,4,2048]{2,1,0:T(4,128)S(1)}, f32[2,4,2048]{2,1,0:T(4,128)}, u32[]{:S(2)}) copy-start(f32[2,4,2048]{2,1,0:T(4,128)} %dy_hbm.1) | copy-start | bytes 196612
  3.5 0.8 %copy-start.4 = (f32[2,4,2048]{2,1,0:T(4,128)S(1)}, f32[2,4,2048]{2,1,0:T(4,128)}, u32[]{:S(2)}) copy-start(f32[2,4,2048]{2,1,0:T(4,128)} %dz_hbm.1) | copy-start | bytes 196612
  4.3 0.8 %copy-start.5 = (s32[2,4,2048]{2,1,0:T(4,128)S(1)}, s32[2,4,2048]{2,1,0:T(4,128)}, u32[]{:S(2)}) copy-start(s32[2,4,2048]{2,1,0:T(4,128)} %sea_hbm.1) | copy-start | bytes 196612
where the time goes:
time: 75.5 us; the launch traced here: 75.1 us
  Pallas kernels  69.2 us (92%)
  local copies, waits for them, and re-layouts  5.82 us (8%)
    pallas_call x1, Pallas kernels, per_device(): pl.pallas_call(kernel, out_shape=jax.ShapeDtypeStruct(shape, F32), in_spe...  69.2 us
    unnamed x13, local copies, waits for them, and re-layouts  5.82 us

commit v1 on v0

--- a/solution.py
+++ b/solution.py
@@ -10,6 +10,7 @@
 MESH = pl.DeviceIdType.MESH
 F32 = jnp.float32
 LEVELS, HALF, TILES, BLOCK, ROWS = 16, 1024, 8, 16, 128
+GROUP = 4
 STRIDES = (1, 2, 4, 8, 16, 32, 64, 128, 256, 512, 1024)
 TO_COLUMNS, TO_LINES, COUPLINGS, NEXT_ROW, REDUCED, LATITUDE, BACK_COLUMNS, BACK_ROWS = 0, 1, 2, 3, 4, 5, 9, 10
 
@@ -203,27 +204,29 @@
     before = (mine + 7) % 8
     send(n_send, n_recv, NEXT_ROW, at(before // 2, zl, before % 2, x, zh))
 
-    def longitude_factor(part_, carry):
-        base = pl.multiple_of(part_ * 64, 64)
-        k = [c_recv[0, pl.ds(base + 8 * j, 8), :] for j in range(TILES)]
-        e = [jnp.ones((8, 128), F32)] * TILES
+    def longitude_factor(step, carry):
+        bases = [pl.multiple_of(step * (64 * GROUP), 64) + 64 * g for g in range(GROUP)]
+        k = [[c_recv[0, pl.ds(base + 8 * j, 8), :] for j in range(TILES)] for base in bases]
+        e = [[jnp.ones((8, 128), F32)] * TILES for _ in bases]
         for i, stride in enumerate(STRIDES):
-            k_east = from_east(k, stride, lane)
-            inv = [1.0 / (a + (b + c)) for a, b, c in zip(e, k, k_east)]
-            plus = [a * b for a, b in zip(k_east, inv)]
-            minus = [a * b for a, b in zip(k, inv)]
+            for g, base in enumerate(bases):
+                k_east = from_east(k[g], stride, lane)
+                inv = [1.0 / (a + (b + c)) for a, b, c in zip(e[g], k[g], k_east)]
+                plus = [a * b for a, b in zip(k_east, inv)]
+                minus = [a * b for a, b in zip(k[g], inv)]
+                for j in range(TILES):
+                    x_factor[i, 0, pl.ds(base + 8 * j, 8), :] = plus[j]
+                    x_factor[i, 1, pl.ds(base + 8 * j, 8), :] = minus[j]
+                west = from_west([a * b for a, b in zip(plus, e[g])], stride, lane)
+                east = from_east([a * b for a, b in zip(minus, e[g])], stride, lane)
+                k[g] = from_west([a * b for a, b in zip(plus, k[g])], stride, lane)
+                e[g] = [a + (b + c) for a, b, c in zip(e[g], west, east)]
+        for g, base in enumerate(bases):
             for j in range(TILES):
-                x_factor[i, 0, pl.ds(base + 8 * j, 8), :] = plus[j]
-                x_factor[i, 1, pl.ds(base + 8 * j, 8), :] = minus[j]
-            west = from_west([a * b for a, b in zip(plus, e)], stride, lane)
-            east = from_east([a * b for a, b in zip(minus, e)], stride, lane)
-            k = from_west([a * b for a, b in zip(plus, k)], stride, lane)
-            e = [a + (b + c) for a, b, c in zip(e, west, east)]
-        for j in range(TILES):
-            x_last[pl.ds(base + 8 * j, 8), :] = 1.0 / e[j]
+                x_last[pl.ds(base + 8 * j, 8), :] = 1.0 / e[g][j]
         return carry
 
-    lax.fori_loop(0, 4, longitude_factor, 0)
+    lax.fori_loop(0, 4 // GROUP, longitude_factor, 0)
 
     wait(n_recv, recv_sem.at[NEXT_ROW])
     for half in range(2):
@@ -266,18 +269,21 @@
         send(r_all.at[mine], r_all.at[mine], REDUCED, target)
 
     def longitude_solve(source):
-        def one(part_, carry):
-            base = pl.multiple_of(part_ * 64, 64)
-            r = [source[pl.ds(base + 8 * j, 8), :] for j in range(TILES)]
+        def one(step, carry):
+            bases = [pl.multiple_of(step * (64 * GROUP), 64) + 64 * g for g in range(GROUP)]
+            r = [[source[pl.ds(base + 8 * j, 8), :] for j in range(TILES)] for base in bases]
             for i, stride in enumerate(STRIDES):
-                west = from_west([x_factor[i, 0, pl.ds(base + 8 * j, 8), :] * r[j] for j in range(TILES)], stride, lane)
-                east = from_east([x_factor[i, 1, pl.ds(base + 8 * j, 8), :] * r[j] for j in range(TILES)], stride, lane)
-                r = [a + (b + c) for a, b, c in zip(r, west, east)]
-            for j in range(TILES):
-                grid[pl.ds(base + 8 * j, 8), :] = r[j] * x_last[pl.ds(base + 8 * j, 8), :]
+                for g, base in enumerate(bases):
+                    plus = [x_factor[i, 0, pl.ds(base + 8 * j, 8), :] * r[g][j] for j in range(TILES)]
+                    minus = [x_factor[i, 1, pl.ds(base + 8 * j, 8), :] * r[g][j] for j in range(TILES)]
+                    west, east = from_west(plus, stride, lane), from_east(minus, stride, lane)
+                    r[g] = [a + (b + c) for a, b, c in zip(r[g], west, east)]
+            for g, base in enumerate(bases):
+                for j in range(TILES):
+                    grid[pl.ds(base + 8 * j, 8), :] = r[g][j] * x_last[pl.ds(base + 8 * j, 8), :]
             return carry
 
-        lax.fori_loop(0, 4, one, 0)
+        lax.fori_loop(0, 4 // GROUP, one, 0)
 
     def reduced_inverse():
         for half in range(2):
@@ -463,7 +469,7 @@
             pltpu.SemaphoreType.DMA((6,)), pltpu.SemaphoreType.DMA((11,)), pltpu.SemaphoreType.DMA((11,)),
         ],
         compiler_params=pltpu.CompilerParams(
-            collective_id=0, has_side_effects=True, vmem_limit_bytes=32 * 1024 * 1024
+            collective_id=0, has_side_effects=True, vmem_limit_bytes=60 * 1024 * 1024
         ),
         name="covariance",
     )(increment, deviations, diffuse_x, diffuse_y, diffuse_z, sea_mask)

time: 75.5 us -> 62.5 us (0.83)
  Pallas kernels: 69.2 us -> 60.5 us
  local copies, waits for them, and re-layouts: 5.82 us -> 1.57 us
    pallas_call x1, Pallas kernels: 69.2 us -> 60.5 us  [per_device(): pl.pallas_call(kernel, out_shape=jax.ShapeDtypeStruct(shape, F32), in_spe...]
    unnamed x13 -> x1, local copies, waits for them, and re-layouts: 5.82 us -> 1.57 us
where the time goes in v1:
time: 62.5 us; the launch traced here: 62.1 us
  Pallas kernels  60.5 us (97%)
  local copies, waits for them, and re-layouts  1.57 us (3%)
    pallas_call x1, Pallas kernels, per_device(): pl.pallas_call(kernel, out_shape=jax.ShapeDtypeStruct(shape, F32), in_spe...  60.5 us
    unnamed x1, local copies, waits for them, and re-layouts  1.57 us

profile of v1, /device:TPU:32, one launch (start us, length us, event | category | flops | bytes accessed | tf_op | source)
XLA Modules:
  0.0 62.1 jit_solution(16577951832789057852)
XLA Ops:
  0.0 60.5 %covariance.1 = f32[2,2,4,2048]{3,2,1,0:T(4,128)} custom-call(f32[2,2,4,2048]{3,2,1,0:T(4,128)} %inc_hbm.1, f32[2,2,4,2048]{3,2,1,0:T(4,128)} %dev_hbm.1, f32[2,4,2048]{2,1,0:T(4,128)} %dx_hbm.1, f32[2,4,2048]{2,1,0:T(4,128)} %dy_hbm.1, f32[2,4,2048]{2,1,0:T(4,128)} %dz_hbm.1, s32[2,4,2048]{2,1,0:T(4,128)} %sea_hbm.1), custom_call_target="tpu_custom_call" | custom-call | tf_op jit(solution)/shard_map/covariance/pallas_call | solution.py:457
  60.5 1.6 %copy.8 = f32[2,2,4,2048]{3,2,1,0:T(4,128)} copy(f32[2,2,4,2048]{3,2,1,0:T(4,128)} %covariance.1) | data formatting | bytes 262144

commit v2 on v0

--- a/solution.py
+++ b/solution.py
@@ -11,7 +11,8 @@
 F32 = jnp.float32
 LEVELS, HALF, TILES, BLOCK, ROWS = 16, 1024, 8, 16, 128
 STRIDES = (1, 2, 4, 8, 16, 32, 64, 128, 256, 512, 1024)
-TO_COLUMNS, TO_LINES, COUPLINGS, NEXT_ROW, REDUCED, LATITUDE, BACK_COLUMNS, BACK_ROWS = 0, 1, 2, 3, 4, 5, 9, 10
+TO_COLUMNS, TO_LINES, COUPLE_X, COUPLE_Y, NEXT_ROW, REDUCED, WEIGHTED = range(7)
+LATITUDE_A, LATITUDE_B, LATITUDE_C, BACK_COLUMNS, BACK_ROWS = range(7, 12)
 
 
 def swap_halves(tile):
@@ -47,8 +48,8 @@
 def kernel(
     inc_hbm, dev_hbm, dx_hbm, dy_hbm, dz_hbm, sea_hbm, out_ref,
     inc, dev, dx, dy, dz, mask, scale,
-    z_send, z_recv, z_factor, z_out, g_recv, c_send, c_recv, n_send, n_recv,
-    x_factor, x_last, y_factor, r_all, inverse, y_all, grid, zb_recv, zb_out, r_recv,
+    z_send, z_recv, z_factor, z_out, g_recv, cx_send, cx_recv, cy_send, cy_recv, n_send, n_recv,
+    x_factor, x_last, y_factor, r_all, w_all, inverse, y_all, f_all, grid, zb_recv, zb_out, r_recv,
     in_sem, send_sem, recv_sem,
 ):
     lat, lev = lax.axis_index("lat"), lax.axis_index("lev")
@@ -122,8 +123,8 @@
         west[0] = jnp.where((lane == 0) & (sublane < 4), 0.0, west[0])
         couple_x, couple_y = tiles_of(paired(dx[l])), tiles_of(paired(dy[l]))
         for j in range(TILES):
-            c_send[l, 0, 8 * j : 8 * j + 8, :] = couple_x[j] * sea_tiles[j] * west[j]
-            c_send[l, 1, 8 * j : 8 * j + 8, :] = couple_y[j] * sea_tiles[j]
+            cx_send[l, 8 * j : 8 * j + 8, :] = couple_x[j] * sea_tiles[j] * west[j]
+            cy_send[l, 8 * j : 8 * j + 8, :] = couple_y[j] * sea_tiles[j]
 
     pl.semaphore_wait(barrier, len(greeted))
 
@@ -133,15 +134,16 @@
             send(z_send.at[t, j], z_recv.at[lev], TO_COLUMNS, at(y, zf, core, j, t))
     part = (zl % 2) * 2 + core
     lines_core = zl // 2
-    for l in range(2):
-        zt = 2 * zh + l
-        for b in (1, 0):
-            target = at(y, zt, lines_core, x, (zh + b) % 2)
-            src, dst = c_send.at[l], c_recv.at[:, pl.ds(pl.multiple_of(part * 64, 64), 64)]
-            if b == 0:
-                send_or_keep(src, dst, COUPLINGS, target, (zl == zt) & (core == lines_core))
-            else:
-                send(src, dst, COUPLINGS, target)
+    for c_send, c_recv, phase in ((cy_send, cy_recv, COUPLE_Y), (cx_send, cx_recv, COUPLE_X)):
+        for l in range(2):
+            zt = 2 * zh + l
+            for b in (1, 0):
+                target = at(y, zt, lines_core, x, (zh + b) % 2)
+                src, dst = c_send.at[l], c_recv.at[pl.ds(pl.multiple_of(part * 64, 64), 64)]
+                if b == 0:
+                    send_or_keep(src, dst, phase, target, (zl == zt) & (core == lines_core))
+                else:
+                    send(src, dst, phase, target)
 
     def solve_levels(take, put):
         upper, lower = take(0), take(15)
@@ -193,42 +195,43 @@
             else:
                 send(src, dst, TO_LINES, target)
 
-    wait(c_recv, recv_sem.at[COUPLINGS])
+    wait(cy_recv, recv_sem.at[COUPLE_Y])
 
     def row_at(i, half):
         return pl.ds((i // 4) * 64 + (i % 4) + 32 * half, 8, stride=4)
 
     for half in range(2):
-        n_send[8 * half : 8 * half + 8, :] = c_recv[1, row_at(0, half), :]
+        n_send[8 * half : 8 * half + 8, :] = cy_recv[row_at(0, half), :]
     before = (mine + 7) % 8
     send(n_send, n_recv, NEXT_ROW, at(before // 2, zl, before % 2, x, zh))
 
-    def longitude_factor(part_, carry):
-        base = pl.multiple_of(part_ * 64, 64)
-        k = [c_recv[0, pl.ds(base + 8 * j, 8), :] for j in range(TILES)]
-        e = [jnp.ones((8, 128), F32)] * TILES
-        for i, stride in enumerate(STRIDES):
-            k_east = from_east(k, stride, lane)
-            inv = [1.0 / (a + (b + c)) for a, b, c in zip(e, k, k_east)]
-            plus = [a * b for a, b in zip(k_east, inv)]
-            minus = [a * b for a, b in zip(k, inv)]
-            for j in range(TILES):
-                x_factor[i, 0, pl.ds(base + 8 * j, 8), :] = plus[j]
-                x_factor[i, 1, pl.ds(base + 8 * j, 8), :] = minus[j]
-            west = from_west([a * b for a, b in zip(plus, e)], stride, lane)
-            east = from_east([a * b for a, b in zip(minus, e)], stride, lane)
-            k = from_west([a * b for a, b in zip(plus, k)], stride, lane)
-            e = [a + (b + c) for a, b, c in zip(e, west, east)]
-        for j in range(TILES):
-            x_last[pl.ds(base + 8 * j, 8), :] = 1.0 / e[j]
-        return carry
-
-    lax.fori_loop(0, 4, longitude_factor, 0)
+    ring = []
+    for k in (4, 5, 3, 2, 6, 7, 1):
+        block = (mine + k) % 8
+        ring.append(at(block // 2, zl, block % 2, x, zh))
+
+    row = (mine * BLOCK + lax.broadcasted_iota(jnp.int32, (BLOCK, 128), 0)).astype(F32)
+    weight = jnp.cos((-78.0 + 166.0 * (row + 0.5) / ROWS) * (math.pi / 180.0))
+    inner = range(1, BLOCK)
+
+    def total(terms):
+        while len(terms) > 1:
+            terms = [sum(terms[i : i + 2][1:], terms[i]) for i in range(0, len(terms), 2)]
+        return terms[0]
+
+    def solve_inner(rows, spot):
+        here, held = None, [None] * BLOCK
+        for i in inner:
+            here = rows[i] if i == 1 else rows[i] + y_factor[0, i - 1, spot, :] * here
+            held[i] = y_factor[1, i, spot, :] * here
+        for i in range(BLOCK - 2, 0, -1):
+            held[i] = held[i] + y_factor[0, i, spot, :] * held[i + 1]
+        return held
 
     wait(n_recv, recv_sem.at[NEXT_ROW])
     for half in range(2):
         spot = pl.ds(8 * half, 8)
-        faces = [c_recv[1, row_at(i, half), :] for i in range(BLOCK)]
+        faces = [cy_recv[row_at(i, half), :] for i in range(BLOCK)]
         north = jnp.where(mine < 7, n_recv[spot, :], 0.0)
         couple = [None] + [
             jnp.where(faces[i - 1] > 0.0, faces[i] if i < BLOCK else north, 0.0) for i in range(1, BLOCK + 1)
@@ -236,12 +239,11 @@
         ground = jnp.ones((8, 128), F32)
         own, link = jnp.ones((8, 128), F32), couple[1]
         to_own, to_next = [None] * BLOCK, [None] * BLOCK
-        for i in range(1, BLOCK):
+        for i in inner:
             inv = 1.0 / (ground + (link + couple[i + 1]))
             to_own[i], to_next[i] = link * inv, couple[i + 1] * inv
-            y_factor[0, i, spot, :] = to_own[i]
-            y_factor[1, i, spot, :] = to_next[i]
-            y_factor[2, i, spot, :] = inv
+            y_factor[0, i, spot, :] = to_next[i]
+            y_factor[1, i, spot, :] = inv
             own = own + to_own[i] * ground
             link = to_own[i] * couple[i + 1]
             beyond = to_next[i] * ground
@@ -250,34 +252,63 @@
         r_all[mine, 1, spot, :] = beyond
         r_all[mine, 2, spot, :] = link
         left, right = to_own[15], to_next[15]
-        y_factor[3, 15, spot, :] = left
-        y_factor[4, 15, spot, :] = right
+        y_factor[2, 15, spot, :] = left
+        y_factor[3, 15, spot, :] = right
         for i in range(BLOCK - 2, 0, -1):
             left = to_own[i] + to_next[i] * left
             right = to_next[i] * right
-            y_factor[3, i, spot, :] = left
-            y_factor[4, i, spot, :] = right
-
-    ring = []
-    for k in (4, 5, 3, 2, 6, 7, 1):
-        block = (mine + k) % 8
-        ring.append(at(block // 2, zl, block % 2, x, zh))
+            y_factor[2, i, spot, :] = left
+            y_factor[3, i, spot, :] = right
     for target in ring:
         send(r_all.at[mine], r_all.at[mine], REDUCED, target)
 
+    for half in range(2):
+        spot = pl.ds(8 * half, 8)
+        sides = [[None] + [y_factor[2 + k, i, spot, :] for i in inner] for k in range(2)]
+        loaded = [[None] + [side[i] * weight[i : i + 1, :] for i in inner] for side in sides]
+        w_all[mine, 0, spot, :] = weight[0:1, :] + total([sides[0][i] * loaded[0][i] for i in inner])
+        w_all[mine, 1, spot, :] = total([sides[0][i] * loaded[1][i] for i in inner])
+        w_all[mine, 2, spot, :] = total([sides[1][i] * loaded[1][i] for i in inner])
+        for k in range(2):
+            twice = solve_inner(loaded[k], spot)
+            for i in inner:
+                y_factor[4 + k, i, spot, :] = twice[i]
+
+    wait(cx_recv, recv_sem.at[COUPLE_X])
+
+    def bases():
+        return [64 * part_ for part_ in range(4)]
+
+    k = [[cx_recv[base + 8 * j : base + 8 * j + 8, :] for j in range(TILES)] for base in bases()]
+    e = [[jnp.ones((8, 128), F32)] * TILES for _ in bases()]
+    for i, stride in enumerate(STRIDES):
+        for g, base in enumerate(bases()):
+            k_east = from_east(k[g], stride, lane)
+            inv = [1.0 / (a + (b + c)) for a, b, c in zip(e[g], k[g], k_east)]
+            plus = [a * b for a, b in zip(k_east, inv)]
+            minus = [a * b for a, b in zip(k[g], inv)]
+            for j in range(TILES):
+                x_factor[i, 0, base + 8 * j : base + 8 * j + 8, :] = plus[j]
+                x_factor[i, 1, base + 8 * j : base + 8 * j + 8, :] = minus[j]
+            west = from_west([a * b for a, b in zip(plus, e[g])], stride, lane)
+            east = from_east([a * b for a, b in zip(minus, e[g])], stride, lane)
+            k[g] = from_west([a * b for a, b in zip(plus, k[g])], stride, lane)
+            e[g] = [a + (b + c) for a, b, c in zip(e[g], west, east)]
+    for g, base in enumerate(bases()):
+        for j in range(TILES):
+            x_last[base + 8 * j : base + 8 * j + 8, :] = 1.0 / e[g][j]
+
     def longitude_solve(source):
-        def one(part_, carry):
-            base = pl.multiple_of(part_ * 64, 64)
-            r = [source[pl.ds(base + 8 * j, 8), :] for j in range(TILES)]
-            for i, stride in enumerate(STRIDES):
-                west = from_west([x_factor[i, 0, pl.ds(base + 8 * j, 8), :] * r[j] for j in range(TILES)], stride, lane)
-                east = from_east([x_factor[i, 1, pl.ds(base + 8 * j, 8), :] * r[j] for j in range(TILES)], stride, lane)
-                r = [a + (b + c) for a, b, c in zip(r, west, east)]
+        r = [[source[base + 8 * j : base + 8 * j + 8, :] for j in range(TILES)] for base in bases()]
+        for i, stride in enumerate(STRIDES):
+            for g, base in enumerate(bases()):
+                plus = [x_factor[i, 0, base + 8 * j : base + 8 * j + 8, :] * r[g][j] for j in range(TILES)]
+                minus = [x_factor[i, 1, base + 8 * j : base + 8 * j + 8, :] * r[g][j] for j in range(TILES)]
+                west, east = from_west(plus, stride, lane), from_east(minus, stride, lane)
+                r[g] = [a + (b + c) for a, b, c in zip(r[g], west, east)]
+        for g, base in enumerate(bases()):
             for j in range(TILES):
-                grid[pl.ds(base + 8 * j, 8), :] = r[j] * x_last[pl.ds(base + 8 * j, 8), :]
-            return carry
-
-        lax.fori_loop(0, 4, one, 0)
+                grid[base + 8 * j : base + 8 * j + 8, :] = r[g][j] * x_last[base + 8 * j : base + 8 * j + 8, :]
 
     def reduced_inverse():
         for half in range(2):
@@ -289,98 +320,135 @@
             below, above = [ground[0]], [None] * 7 + [jnp.zeros((8, 128), F32)]
             north, south = [None] * 8, [None] * 8
             for b in range(7):
-                north[b] = link[b] / (below[b] + link[b])
+                inv = 1.0 / (below[b] + link[b])
+                north[b] = link[b] * inv
+                inverse[4, b, spot, :] = north[b]
+                inverse[5, b, spot, :] = inv
                 below.append(ground[b + 1] + north[b] * below[b])
+            inverse[5, 7, spot, :] = 1.0 / below[7]
             for b in range(7, 0, -1):
-                total = ground[b] + above[b]
-                south[b] = link[b - 1] / (total + link[b - 1])
-                above[b - 1] = south[b] * total
+                whole = ground[b] + above[b]
+                south[b] = link[b - 1] / (whole + link[b - 1])
+                above[b - 1] = south[b] * whole
             for which in range(2):
                 spike = mine + which
-                row = [None] * 8
+                row_ = [None] * 8
                 here = jnp.zeros((8, 128), F32)
                 for b in range(7, -1, -1):
                     moved = here if b == 7 else north[b] * here
                     here = jnp.where(spike == b, 1.0 / (below[b] + above[b]), moved)
-                    row[b] = here
+                    row_[b] = here
                 here = jnp.zeros((8, 128), F32)
                 for b in range(8):
                     moved = here if b == 0 else south[b] * here
-                    here = jnp.where(spike < b, moved, row[b])
+                    here = jnp.where(spike < b, moved, row_[b])
                     inverse[which, b, spot, :] = here
 
-    def latitude_solve(rows, step, between=None):
-        held = []
-        for half in range(2):
-            spot = pl.ds(8 * half, 8)
-            own, here = rows(0, half), rows(1, half)
-            mid = [None]
-            for i in range(1, BLOCK):
-                mid.append(y_factor[2, i, spot, :] * here)
-                own = own + y_factor[0, i, spot, :] * here
-                here = y_factor[1, i, spot, :] * here
-                if i + 1 < BLOCK:
-                    here = rows(i + 1, half) + here
-            y_all[step, mine, spot, :] = own
-            y_all[step, mine, pl.ds(16 + 8 * half, 8), :] = here
-            held.append(mid)
+    def weighted_inverse():
+        for half in range(2):
+            spot = pl.ds(8 * half, 8)
+            middle = [w_all[b, 0, spot, :] for b in range(8)]
+            for b in range(1, 8):
+                middle[b] = middle[b] + w_all[b - 1, 2, spot, :]
+            beside = [w_all[b, 1, spot, :] for b in range(7)]
+            for which in range(2):
+                g = [inverse[which, b, spot, :] for b in range(8)]
+                right = [middle[b] * g[b] for b in range(8)]
+                for b in range(7):
+                    right[b] = right[b] + beside[b] * g[b + 1]
+                    right[b + 1] = right[b + 1] + beside[b] * g[b]
+                for b in range(7):
+                    right[b + 1] = right[b + 1] + inverse[4, b, spot, :] * right[b]
+                here = inverse[5, 7, spot, :] * right[7]
+                inverse[2 + which, 7, spot, :] = here
+                for b in range(6, -1, -1):
+                    here = inverse[5, b, spot, :] * right[b] + inverse[4, b, spot, :] * here
+                    inverse[2 + which, b, spot, :] = here
+
+    def rows_of(half):
+        return [grid[row_at(i, half), :] for i in range(BLOCK)]
+
+    def put_rows(half, rows):
+        for i in range(BLOCK):
+            grid[row_at(i, half), :] = rows[i]
+
+    def gathered(everyone, first, half):
+        values = [everyone[b, pl.ds(16 * first + 8 * half, 8), :] for b in range(8)]
+        for b in range(1, 8):
+            values[b] = values[b] + everyone[b - 1, pl.ds(16 * (first + 1) + 8 * half, 8), :]
+        return values
+
+    def applied(which, values, spot):
+        return [inverse[which, b, spot, :] * values[b] for b in range(8)]
+
+    def tell(everyone, phase):
         for target in ring:
-            send(y_all.at[step, mine], y_all.at[step, mine], LATITUDE + step, target)
-        for half in range(2):
-            spot = pl.ds(8 * half, 8)
-            for i in range(BLOCK - 2, 0, -1):
-                held[half][i] = held[half][i] + y_factor[1, i, spot, :] * held[half][i + 1]
+            send(everyone.at[mine], everyone.at[mine], phase, target)
+
+    def latitude_solve(everyone, phase, behind=None, between=None):
+        inside = []
+        for half in range(2):
+            spot = pl.ds(8 * half, 8)
+            rows = rows_of(half)
+            own = total([rows[0]] + [y_factor[2, i, spot, :] * rows[i] for i in inner])
+            beyond = total([y_factor[3, i, spot, :] * rows[i] for i in inner])
+            everyone[mine, spot, :] = own
+            everyone[mine, pl.ds(16 + 8 * half, 8), :] = beyond
+        tell(everyone, phase)
+        if behind is not None:
+            behind()
+        for half in range(2):
+            inside.append(solve_inner(rows_of(half), pl.ds(8 * half, 8)))
         if between is not None:
             between()
-        wait(y_all.at[step, pl.ds(0, 7)], recv_sem.at[LATITUDE + step])
-        result = []
-        for half in range(2):
-            spot = pl.ds(8 * half, 8)
-            ends = []
-            right = []
-            for b in range(8):
-                value = y_all[step, b, spot, :]
-                if b > 0:
-                    value = value + y_all[step, b - 1, pl.ds(16 + 8 * half, 8), :]
-                right.append(value)
-            for which in range(2):
-                terms = [inverse[which, b, spot, :] * right[b] for b in range(8)]
-                while len(terms) > 1:
-                    terms = [a + b for a, b in zip(terms[::2], terms[1::2])]
-                ends.append(terms[0])
-            result.append(
-                [ends[0]]
-                + [
-                    held[half][i] + (y_factor[3, i, spot, :] * ends[0] + y_factor[4, i, spot, :] * ends[1])
-                    for i in range(1, BLOCK)
-                ]
-            )
-        return result
-
-    def from_grid(i, half):
-        return grid[row_at(i, half), :]
-
-    def to_grid(result):
-        for half in range(2):
-            for i in range(BLOCK):
-                grid[row_at(i, half), :] = result[half][i]
+        wait(everyone.at[pl.ds(0, 7)], recv_sem.at[phase])
+        for half in range(2):
+            spot = pl.ds(8 * half, 8)
+            right = gathered(everyone, 0, half)
+            first, last = (total(applied(which, right, spot)) for which in range(2))
+            put_rows(half, [first] + [
+                inside[half][i] + (y_factor[2, i, spot, :] * first + y_factor[3, i, spot, :] * last) for i in inner
+            ])
+
+    def latitude_pair(everyone, phase):
+        inside = []
+        for half in range(2):
+            spot = pl.ds(8 * half, 8)
+            rows = rows_of(half)
+            for k in range(4):
+                terms = [y_factor[2 + k, i, spot, :] * rows[i] for i in inner]
+                everyone[mine, pl.ds(16 * k + 8 * half, 8), :] = total(([rows[0]] if k == 0 else []) + terms)
+        tell(everyone, phase)
+        for half in range(2):
+            spot = pl.ds(8 * half, 8)
+            once = solve_inner(rows_of(half), spot)
+            inside.append(solve_inner([None] + [once[i] * weight[i : i + 1, :] for i in inner], spot))
+        wait(w_all.at[pl.ds(0, 7)], recv_sem.at[WEIGHTED])
+        weighted_inverse()
+        wait(everyone.at[pl.ds(0, 7)], recv_sem.at[phase])
+        for half in range(2):
+            spot = pl.ds(8 * half, 8)
+            right, more = gathered(everyone, 0, half), gathered(everyone, 2, half)
+            ends = [total(applied(which, right, spot)) for which in range(2)]
+            ends += [total(applied(2 + k, right, spot) + applied(k, more, spot)) for k in range(2)]
+            put_rows(half, [ends[2]] + [
+                inside[half][i]
+                + (y_factor[4, i, spot, :] * ends[0] + y_factor[5, i, spot, :] * ends[1])
+                + (y_factor[2, i, spot, :] * ends[2] + y_factor[3, i, spot, :] * ends[3])
+                for i in inner
+            ])
 
     def first_between():
         wait(r_all.at[pl.ds(0, 7)], recv_sem.at[REDUCED])
         reduced_inverse()
 
-    row = (mine * BLOCK + lax.broadcasted_iota(jnp.int32, (BLOCK, 128), 0)).astype(F32)
-    weight = jnp.cos((-78.0 + 166.0 * (row + 0.5) / ROWS) * (math.pi / 180.0))
-
     wait(g_recv, recv_sem.at[TO_LINES])
     longitude_solve(g_recv)
-    to_grid(latitude_solve(from_grid, 0, first_between))
+    latitude_solve(y_all.at[0], LATITUDE_A, lambda: tell(w_all, WEIGHTED), first_between)
     longitude_solve(grid)
-    forward = latitude_solve(from_grid, 1)
-    weighted = [[forward[half][i] * weight[i : i + 1, :] for i in range(BLOCK)] for half in range(2)]
-    to_grid(latitude_solve(lambda i, half: weighted[half][i], 2))
+    latitude_pair(f_all, LATITUDE_B)
     longitude_solve(grid)
-    to_grid(latitude_solve(from_grid, 3))
+    latitude_solve(y_all.at[1], LATITUDE_C)
     longitude_solve(grid)
 
     level = x * 4 + zl
@@ -416,13 +484,13 @@
                 out_ref[t, l, :, HALF + 128 * j : HALF + 128 * j + 128] = tile[4:]
 
     wait(z_send.at[:, :, :, :], send_sem.at[TO_COLUMNS])
-    for l in range(2):
-        wait(c_send.at[l], send_sem.at[COUPLINGS])
-        kept = (zl == 2 * zh + l) & (core == lines_core)
-
-        @pl.when(jnp.logical_not(kept))
-        def _():
-            wait(c_send.at[l], send_sem.at[COUPLINGS])
+    for c_send, phase in ((cy_send, COUPLE_Y), (cx_send, COUPLE_X)):
+        for l in range(2):
+            wait(c_send.at[l], send_sem.at[phase])
+
+            @pl.when(jnp.logical_not((zl == 2 * zh + l) & (core == lines_core)))
+            def _():
+                wait(c_send.at[l], send_sem.at[phase])
 
     wait(z_out.at[pl.ds(0, 15)], send_sem.at[TO_LINES])
 
@@ -432,8 +500,10 @@
 
     wait(n_send, send_sem.at[NEXT_ROW])
     wait(r_all.at[pl.ds(0, 7)], send_sem.at[REDUCED])
-    for step in range(4):
-        wait(y_all.at[step, pl.ds(0, 7)], send_sem.at[LATITUDE + step])
+    wait(w_all.at[pl.ds(0, 7)], send_sem.at[WEIGHTED])
+    wait(y_all.at[0, pl.ds(0, 7)], send_sem.at[LATITUDE_A])
+    wait(f_all.at[pl.ds(0, 7)], send_sem.at[LATITUDE_B])
+    wait(y_all.at[1, pl.ds(0, 7)], send_sem.at[LATITUDE_C])
     wait(zb_recv.at[pl.ds(0, 15)], send_sem.at[BACK_COLUMNS])
     base = (zl - 2 * core + 2) % 4
 
@@ -457,13 +527,13 @@
             vmem(*shape), vmem(*shape), vmem(*plane), vmem(*plane), vmem(*plane), pltpu.VMEM(plane, jnp.int32),
             vmem(2, 2, 64, 128),
             vmem(2, 4, 2, 2, 16, 128), vmem(8, 2, 2, 16, 128), vmem(2, 16, 16, 128), vmem(16, 16, 128),
-            vmem(256, 128), vmem(2, 2, 64, 128), vmem(2, 256, 128), vmem(16, 128), vmem(16, 128),
-            vmem(11, 2, 256, 128), vmem(256, 128), vmem(5, 16, 16, 128), vmem(8, 3, 16, 128), vmem(2, 8, 16, 128),
-            vmem(4, 8, 32, 128), vmem(256, 128), vmem(16, 16, 128), vmem(16, 16, 128), vmem(2, 2, 64, 128),
-            pltpu.SemaphoreType.DMA((6,)), pltpu.SemaphoreType.DMA((11,)), pltpu.SemaphoreType.DMA((11,)),
+            vmem(256, 128), vmem(2, 64, 128), vmem(256, 128), vmem(2, 64, 128), vmem(256, 128), vmem(16, 128), vmem(16, 128),
+            vmem(11, 2, 256, 128), vmem(256, 128), vmem(6, 16, 16, 128), vmem(8, 3, 16, 128), vmem(8, 3, 16, 128),
+            vmem(6, 8, 16, 128), vmem(2, 8, 32, 128), vmem(8, 64, 128), vmem(256, 128), vmem(16, 16, 128), vmem(16, 16, 128), vmem(2, 2, 64, 128),
+            pltpu.SemaphoreType.DMA((6,)), pltpu.SemaphoreType.DMA((12,)), pltpu.SemaphoreType.DMA((12,)),
         ],
         compiler_params=pltpu.CompilerParams(
-            collective_id=0, has_side_effects=True, vmem_limit_bytes=32 * 1024 * 1024
+            collective_id=0, has_side_effects=True, vmem_limit_bytes=60 * 1024 * 1024
         ),
         name="covariance",
     )(increment, deviations, diffuse_x, diffuse_y, diffuse_z, sea_mask)

time: 75.5 us -> 60.2 us (0.80)
  Pallas kernels: 69.2 us -> 58.3 us
  local copies, waits for them, and re-layouts: 5.82 us -> 1.57 us
    pallas_call x1, Pallas kernels: 69.2 us -> 58.3 us  [per_device(): pl.pallas_call(kernel, out_shape=jax.ShapeDtypeStruct(shape, F32), in_spe...]
    unnamed x13 -> x1, local copies, waits for them, and re-layouts: 5.82 us -> 1.57 us
where the time goes in v2:
time: 60.2 us; the launch traced here: 59.9 us
  Pallas kernels  58.3 us (97%)
  local copies, waits for them, and re-layouts  1.57 us (3%)
    pallas_call x1, Pallas kernels, per_device(): pl.pallas_call(kernel, out_shape=jax.ShapeDtypeStruct(shape, F32), in_spe...  58.3 us
    unnamed x1, local copies, waits for them, and re-layouts  1.57 us

profile of v2, /device:TPU:32, one launch (start us, length us, event | category | flops | bytes accessed | tf_op | source)
XLA Modules:
  0.0 59.9 jit_solution(15102668444312286331)
XLA Ops:
  0.0 58.3 %covariance.1 = f32[2,2,4,2048]{3,2,1,0:T(4,128)} custom-call(f32[2,2,4,2048]{3,2,1,0:T(4,128)} %inc_hbm.1, f32[2,2,4,2048]{3,2,1,0:T(4,128)} %dev_hbm.1, f32[2,4,2048]{2,1,0:T(4,128)} %dx_hbm.1, f32[2,4,2048]{2,1,0:T(4,128)} %dy_hbm.1, f32[2,4,2048]{2,1,0:T(4,128)} %dz_hbm.1, s32[2,4,2048]{2,1,0:T(4,128)} %sea_hbm.1), custom_call_target="tpu_custom_call" | custom-call | tf_op jit(solution)/shard_map/covariance/pallas_call | solution.py:521
  58.3 1.6 %copy.8 = f32[2,2,4,2048]{3,2,1,0:T(4,128)} copy(f32[2,2,4,2048]{3,2,1,0:T(4,128)} %covariance.1) | data formatting | bytes 262144

commit v3 on v2

--- a/solution.py
+++ b/solution.py
@@ -61,6 +61,10 @@
 
     def at(y_, zl_, core_, x_, zh_):
         return {"lat": y_ * 8 + zl_ * 2 + core_, "lev": x_ * 2 + zh_}
+
+    def level_at(x_, zl_):
+        inner = ((zl_ + 1) // 2) % 2
+        return x_ * 4 + 2 * ((zh + 1 + inner) % 2) + zl_ // 2
 
     def send(src, dst, phase, target):
         pltpu.make_async_remote_copy(
@@ -136,8 +140,8 @@
     lines_core = zl // 2
     for c_send, c_recv, phase in ((cy_send, cy_recv, COUPLE_Y), (cx_send, cx_recv, COUPLE_X)):
         for l in range(2):
-            zt = 2 * zh + l
             for b in (1, 0):
+                zt = 3 * l if b else 1 + l
                 target = at(y, zt, lines_core, x, (zh + b) % 2)
                 src, dst = c_send.at[l], c_recv.at[pl.ds(pl.multiple_of(part * 64, 64), 64)]
                 if b == 0:
@@ -187,7 +191,7 @@
     for a in (2, 1, 3, 0):
         for b in (3, 1, 2, 0):
             x_, zl_ = (x + a) % 4, (zl + b) % 4
-            src = z_out.at[x_ * 4 + zl_]
+            src = z_out.at[level_at(x_, zl_)]
             dst = g_recv.at[pl.ds(pl.multiple_of(from_part * 64 + x * 16, 16), 16)]
             target = at(y, zl_, from_core, x_, zh)
             if a == 0 and b == 0:
@@ -262,18 +266,6 @@
     for target in ring:
         send(r_all.at[mine], r_all.at[mine], REDUCED, target)
 
-    for half in range(2):
-        spot = pl.ds(8 * half, 8)
-        sides = [[None] + [y_factor[2 + k, i, spot, :] for i in inner] for k in range(2)]
-        loaded = [[None] + [side[i] * weight[i : i + 1, :] for i in inner] for side in sides]
-        w_all[mine, 0, spot, :] = weight[0:1, :] + total([sides[0][i] * loaded[0][i] for i in inner])
-        w_all[mine, 1, spot, :] = total([sides[0][i] * loaded[1][i] for i in inner])
-        w_all[mine, 2, spot, :] = total([sides[1][i] * loaded[1][i] for i in inner])
-        for k in range(2):
-            twice = solve_inner(loaded[k], spot)
-            for i in inner:
-                y_factor[4 + k, i, spot, :] = twice[i]
-
     wait(cx_recv, recv_sem.at[COUPLE_X])
 
     def bases():
@@ -438,20 +430,34 @@
                 for i in inner
             ])
 
+    def weighted_block():
+        for half in range(2):
+            spot = pl.ds(8 * half, 8)
+            sides = [[None] + [y_factor[2 + k, i, spot, :] for i in inner] for k in range(2)]
+            loaded = [[None] + [side[i] * weight[i : i + 1, :] for i in inner] for side in sides]
+            w_all[mine, 0, spot, :] = weight[0:1, :] + total([sides[0][i] * loaded[0][i] for i in inner])
+            w_all[mine, 1, spot, :] = total([sides[0][i] * loaded[1][i] for i in inner])
+            w_all[mine, 2, spot, :] = total([sides[1][i] * loaded[1][i] for i in inner])
+            for k in range(2):
+                twice = solve_inner(loaded[k], spot)
+                for i in inner:
+                    y_factor[4 + k, i, spot, :] = twice[i]
+        tell(w_all, WEIGHTED)
+
     def first_between():
         wait(r_all.at[pl.ds(0, 7)], recv_sem.at[REDUCED])
         reduced_inverse()
 
     wait(g_recv, recv_sem.at[TO_LINES])
     longitude_solve(g_recv)
-    latitude_solve(y_all.at[0], LATITUDE_A, lambda: tell(w_all, WEIGHTED), first_between)
+    latitude_solve(y_all.at[0], LATITUDE_A, weighted_block, first_between)
     longitude_solve(grid)
     latitude_pair(f_all, LATITUDE_B)
     longitude_solve(grid)
     latitude_solve(y_all.at[1], LATITUDE_C)
     longitude_solve(grid)
 
-    level = x * 4 + zl
+    level = level_at(x, zl)
     for a in (2, 1, 3, 0):
         x_ = (x + a) % 4
         for b in range(4):
@@ -488,7 +494,7 @@
         for l in range(2):
             wait(c_send.at[l], send_sem.at[phase])
 
-            @pl.when(jnp.logical_not((zl == 2 * zh + l) & (core == lines_core)))
+            @pl.when(jnp.logical_not((zl == 1 + l) & (core == lines_core)))
             def _():
                 wait(c_send.at[l], send_sem.at[phase])
 

time: 60.2 us -> 57.3 us (0.952)
  Pallas kernels: 58.3 us -> 55.6 us
    pallas_call x1, Pallas kernels: 58.3 us -> 55.6 us  [per_device(): pl.pallas_call(kernel, out_shape=jax.ShapeDtypeStruct(shape, F32), in_spe...]
where the time goes in v3:
time: 57.3 us; the launch traced here: 57.2 us
  Pallas kernels  55.6 us (97%)
  local copies, waits for them, and re-layouts  1.57 us (3%)
    pallas_call x1, Pallas kernels, per_device(): pl.pallas_call(kernel, out_shape=jax.ShapeDtypeStruct(shape, F32), in_spe...  55.6 us
    unnamed x1, local copies, waits for them, and re-layouts  1.57 us

profile of v3, /device:TPU:32, one launch (start us, length us, event | category | flops | bytes accessed | tf_op | source)
XLA Modules:
  0.0 57.2 jit_solution(12403089581754994856)
XLA Ops:
  0.0 55.6 %covariance.1 = f32[2,2,4,2048]{3,2,1,0:T(4,128)} custom-call(f32[2,2,4,2048]{3,2,1,0:T(4,128)} %inc_hbm.1, f32[2,2,4,2048]{3,2,1,0:T(4,128)} %dev_hbm.1, f32[2,4,2048]{2,1,0:T(4,128)} %dx_hbm.1, f32[2,4,2048]{2,1,0:T(4,128)} %dy_hbm.1, f32[2,4,2048]{2,1,0:T(4,128)} %dz_hbm.1, s32[2,4,2048]{2,1,0:T(4,128)} %sea_hbm.1), custom_call_target="tpu_custom_call" | custom-call | tf_op jit(solution)/shard_map/covariance/pallas_call | solution.py:527
  55.6 1.6 %copy.8 = f32[2,2,4,2048]{3,2,1,0:T(4,128)} copy(f32[2,2,4,2048]{3,2,1,0:T(4,128)} %covariance.1) | data formatting | bytes 262144

commit v4 on v3

--- a/solution.py
+++ b/solution.py
@@ -94,16 +94,32 @@
         load.start()
 
     zf = (zl + 2) % 4
-    greeted = [at(y, zf, core, (x + a) % 4, (zh + b) % 2) for a in (2, 1, 3, 0) for b in (0, 1)]
-    greeted += [
-        at(y, (zl + a) % 4, (core + d) % 2, x, (zh + b) % 2)
-        for a in range(4) for b in range(2) for d in range(2)
-        if (a, b, d) != (0, 0, 0) and (a, d) != (2, 0)
-    ]
-    greeted += [at((y + a) % 4, zl, d, x, zh) for a in (2, 1, 3) for d in range(2)]
     barrier = pltpu.get_barrier_semaphore()
-    for target in greeted:
+
+    def greet(target):
         pl.semaphore_signal(barrier, inc=1, device_id=target, device_id_type=MESH)
+
+    for a in (2, 1, 3, 0):
+        for b in (0, 1):
+            greet(at(y, zf, core, (x + a) % 4, (zh + b) % 2))
+
+    @pl.when(zl % 3 == 0)
+    def _():
+        for a in range(2):
+            for d in range(2):
+                greet(at(y, 2 * core + a, d, x, 1 - zh))
+
+    for a in range(2):
+
+        @pl.when(zl != 2 * core + a)
+        def _():
+            for d in range(2):
+                greet(at(y, 2 * core + a, d, x, zh))
+
+    for a in (2, 1, 3):
+        for d in range(2):
+            greet(at((y + a) % 4, zl, d, x, zh))
+    greet(at(y, zl, 1 - core, x, zh))
 
     for load in loads[:4]:
         load.wait()
@@ -130,7 +146,7 @@
             cx_send[l, 8 * j : 8 * j + 8, :] = couple_x[j] * sea_tiles[j] * west[j]
             cy_send[l, 8 * j : 8 * j + 8, :] = couple_y[j] * sea_tiles[j]
 
-    pl.semaphore_wait(barrier, len(greeted))
+    pl.semaphore_wait(barrier, 20)
 
     for a in (2, 1, 3, 0):
         j = (x + a) % 4
@@ -290,7 +306,8 @@
         for j in range(TILES):
             x_last[base + 8 * j : base + 8 * j + 8, :] = 1.0 / e[g][j]
 
-    def longitude_solve(source):
+    def longitude_solve(source, parts=(0, 1, 2, 3)):
+        bases = lambda: [64 * part_ for part_ in parts]
         r = [[source[base + 8 * j : base + 8 * j + 8, :] for j in range(TILES)] for base in bases()]
         for i, stride in enumerate(STRIDES):
             for g, base in enumerate(bases()):
@@ -455,19 +472,20 @@
     latitude_pair(f_all, LATITUDE_B)
     longitude_solve(grid)
     latitude_solve(y_all.at[1], LATITUDE_C)
-    longitude_solve(grid)
 
     level = level_at(x, zl)
-    for a in (2, 1, 3, 0):
-        x_ = (x + a) % 4
-        for b in range(4):
-            zl_, core_ = (2 * core + b // 2 + 2) % 4, b % 2
-            src = grid.at[pl.ds(pl.multiple_of(b * 64 + x_ * 16, 16), 16)]
-            target = at(y, zl_, core_, x_, zh)
-            if a == 0:
-                send_or_keep(src, zb_recv.at[level], BACK_COLUMNS, target, (zl_ == zl) & (core_ == core))
-            else:
-                send(src, zb_recv.at[level], BACK_COLUMNS, target)
+    for first in (0, 2):
+        longitude_solve(grid, (first, first + 1))
+        for a in (2, 1, 3, 0):
+            x_ = (x + a) % 4
+            for b in (first, first + 1):
+                zl_, core_ = (2 * core + b // 2 + 2) % 4, b % 2
+                src = grid.at[pl.ds(pl.multiple_of(b * 64 + x_ * 16, 16), 16)]
+                target = at(y, zl_, core_, x_, zh)
+                if a == 0:
+                    send_or_keep(src, zb_recv.at[level], BACK_COLUMNS, target, (zl_ == zl) & (core_ == core))
+                else:
+                    send(src, zb_recv.at[level], BACK_COLUMNS, target)
     wait(zb_recv, recv_sem.at[BACK_COLUMNS])
 
     def put_last(k, value):

time: 57.3 us -> 57.2 us (level)
  no operation moved by 1% of the time
where the time goes in v4:
time: 57.2 us; the launch traced here: 57.1 us
  Pallas kernels  55.5 us (97%)
  local copies, waits for them, and re-layouts  1.57 us (3%)
    pallas_call x1, Pallas kernels, per_device(): pl.pallas_call(kernel, out_shape=jax.ShapeDtypeStruct(shape, F32), in_spe...  55.5 us
    unnamed x1, local copies, waits for them, and re-layouts  1.57 us

profile of v4, /device:TPU:32, one launch (start us, length us, event | category | flops | bytes accessed | tf_op | source)
XLA Modules:
  0.0 57.1 jit_solution(3738462691454947430)
XLA Ops:
  0.0 55.5 %covariance.1 = f32[2,2,4,2048]{3,2,1,0:T(4,128)} custom-call(f32[2,2,4,2048]{3,2,1,0:T(4,128)} %inc_hbm.1, f32[2,2,4,2048]{3,2,1,0:T(4,128)} %dev_hbm.1, f32[2,4,2048]{2,1,0:T(4,128)} %dx_hbm.1, f32[2,4,2048]{2,1,0:T(4,128)} %dy_hbm.1, f32[2,4,2048]{2,1,0:T(4,128)} %dz_hbm.1, s32[2,4,2048]{2,1,0:T(4,128)} %sea_hbm.1), custom_call_target="tpu_custom_call" | custom-call | tf_op jit(solution)/shard_map/covariance/pallas_call | solution.py:545
  55.5 1.6 %copy.8 = f32[2,2,4,2048]{3,2,1,0:T(4,128)} copy(f32[2,2,4,2048]{3,2,1,0:T(4,128)} %covariance.1) | data formatting | bytes 262144

commit v5 on v4

--- a/solution.py
+++ b/solution.py
@@ -47,7 +47,7 @@
 
 def kernel(
     inc_hbm, dev_hbm, dx_hbm, dy_hbm, dz_hbm, sea_hbm, out_ref,
-    inc, dev, dx, dy, dz, mask, scale,
+    inc, dev, dx, dy, dz, mask, scale, result,
     z_send, z_recv, z_factor, z_out, g_recv, cx_send, cx_recv, cy_send, cy_recv, n_send, n_recv,
     x_factor, x_last, y_factor, r_all, w_all, inverse, y_all, f_all, grid, zb_recv, zb_out, r_recv,
     in_sem, send_sem, recv_sem,
@@ -497,15 +497,18 @@
             x_ = (x + a) % 4
             src = zb_out.at[pl.ds(x_ * 4 + b * 2, 2)]
             dst = r_recv.at[zh, :, pl.ds(pl.multiple_of(x * 16, 16), 16)]
-            send(src, dst, BACK_ROWS, at(y, zf, core, x_, b))
-    wait(r_recv, recv_sem.at[BACK_ROWS])
+            send(src, dst, BACK_ROWS + zh, at(y, zf, core, x_, b))
+    stores = []
     for t in range(2):
+        wait(r_recv.at[t], recv_sem.at[BACK_ROWS + t])
         for l in range(2):
             for j in range(TILES):
                 spot = pl.ds(8 * j, 8)
                 tile = scale[t, l, spot, :] * r_recv[t, l, spot, :]
-                out_ref[t, l, :, 128 * j : 128 * j + 128] = tile[:4]
-                out_ref[t, l, :, HALF + 128 * j : HALF + 128 * j + 128] = tile[4:]
+                result[t, l, :, 128 * j : 128 * j + 128] = tile[:4]
+                result[t, l, :, HALF + 128 * j : HALF + 128 * j + 128] = tile[4:]
+            stores.append(pltpu.make_async_copy(result.at[t, l], out_ref.at[t, l], in_sem.at[2 * t + l]))
+            stores[-1].start()
 
     wait(z_send.at[:, :, :, :], send_sem.at[TO_COLUMNS])
     for c_send, phase in ((cy_send, COUPLE_Y), (cx_send, COUPLE_X)):
@@ -535,7 +538,9 @@
     def _():
         wait(zb_recv.at[15], send_sem.at[BACK_COLUMNS])
 
-    wait(r_recv, send_sem.at[BACK_ROWS])
+    wait(r_recv, send_sem.at[BACK_ROWS + zh])
+    for store in stores:
+        store.wait()
 
 
 def per_device(increment, deviations, diffuse_x, diffuse_y, diffuse_z, sea_mask):
@@ -546,15 +551,15 @@
         kernel,
         out_shape=jax.ShapeDtypeStruct(shape, F32),
         in_specs=[pl.BlockSpec(memory_space=pl.ANY)] * 6,
-        out_specs=pl.BlockSpec(memory_space=pltpu.VMEM),
+        out_specs=pl.BlockSpec(memory_space=pl.ANY),
         scratch_shapes=[
             vmem(*shape), vmem(*shape), vmem(*plane), vmem(*plane), vmem(*plane), pltpu.VMEM(plane, jnp.int32),
-            vmem(2, 2, 64, 128),
+            vmem(2, 2, 64, 128), vmem(*shape),
             vmem(2, 4, 2, 2, 16, 128), vmem(8, 2, 2, 16, 128), vmem(2, 16, 16, 128), vmem(16, 16, 128),
             vmem(256, 128), vmem(2, 64, 128), vmem(256, 128), vmem(2, 64, 128), vmem(256, 128), vmem(16, 128), vmem(16, 128),
             vmem(11, 2, 256, 128), vmem(256, 128), vmem(6, 16, 16, 128), vmem(8, 3, 16, 128), vmem(8, 3, 16, 128),
             vmem(6, 8, 16, 128), vmem(2, 8, 32, 128), vmem(8, 64, 128), vmem(256, 128), vmem(16, 16, 128), vmem(16, 16, 128), vmem(2, 2, 64, 128),
-            pltpu.SemaphoreType.DMA((6,)), pltpu.SemaphoreType.DMA((12,)), pltpu.SemaphoreType.DMA((12,)),
+            pltpu.SemaphoreType.DMA((6,)), pltpu.SemaphoreType.DMA((13,)), pltpu.SemaphoreType.DMA((13,)),
         ],
         compiler_params=pltpu.CompilerParams(
             collective_id=0, has_side_effects=True, vmem_limit_bytes=60 * 1024 * 1024

time: 57.2 us -> 57.1 us (level)
  no operation moved by 1% of the time
where the time goes in v5:
time: 57.1 us; the launch traced here: 57 us
  Pallas kernels  55.5 us (97%)
  local copies, waits for them, and re-layouts  1.57 us (3%)
    pallas_call x1, Pallas kernels, per_device(): pl.pallas_call(kernel, out_shape=jax.ShapeDtypeStruct(shape, F32), in_spe...  55.5 us
    unnamed x1, local copies, waits for them, and re-layouts  1.57 us

profile of v5, /device:TPU:32, one launch (start us, length us, event | category | flops | bytes accessed | tf_op | source)
XLA Modules:
  0.0 57.0 jit_solution(2917717989739699690)
XLA Ops:
  0.0 55.5 %covariance.1 = f32[2,2,4,2048]{3,2,1,0:T(4,128)} custom-call(f32[2,2,4,2048]{3,2,1,0:T(4,128)} %inc_hbm.1, f32[2,2,4,2048]{3,2,1,0:T(4,128)} %dev_hbm.1, f32[2,4,2048]{2,1,0:T(4,128)} %dx_hbm.1, f32[2,4,2048]{2,1,0:T(4,128)} %dy_hbm.1, f32[2,4,2048]{2,1,0:T(4,128)} %dz_hbm.1, s32[2,4,2048]{2,1,0:T(4,128)} %sea_hbm.1), custom_call_target="tpu_custom_call" | custom-call | tf_op jit(solution)/shard_map/covariance/pallas_call | solution.py:550
  55.5 1.6 %copy.8 = f32[2,2,4,2048]{3,2,1,0:T(4,128)} copy(f32[2,2,4,2048]{3,2,1,0:T(4,128)} %covariance.1) | data formatting | bytes 262144

commit v6 on v5

--- a/solution.py
+++ b/solution.py
@@ -151,7 +151,7 @@
     for a in (2, 1, 3, 0):
         j = (x + a) % 4
         for t in range(2):
-            send(z_send.at[t, j], z_recv.at[lev], TO_COLUMNS, at(y, zf, core, j, t))
+            send(z_send.at[(zh + t) % 2, j], z_recv.at[lev], TO_COLUMNS, at(y, zf, core, j, (zh + t) % 2))
     part = (zl % 2) * 2 + core
     lines_core = zl // 2
     for c_send, c_recv, phase in ((cy_send, cy_recv, COUPLE_Y), (cx_send, cx_recv, COUPLE_X)):
@@ -226,9 +226,10 @@
     send(n_send, n_recv, NEXT_ROW, at(before // 2, zl, before % 2, x, zh))
 
     ring = []
-    for k in (4, 5, 3, 2, 6, 7, 1):
-        block = (mine + k) % 8
-        ring.append(at(block // 2, zl, block % 2, x, zh))
+    for a in (2, 1, 3):
+        for d in range(2):
+            ring.append(at((y + a) % 4, zl, (core + d) % 2, x, zh))
+    ring.append(at(y, zl, 1 - core, x, zh))
 
     row = (mine * BLOCK + lax.broadcasted_iota(jnp.int32, (BLOCK, 128), 0)).astype(F32)
     weight = jnp.cos((-78.0 + 166.0 * (row + 0.5) / ROWS) * (math.pi / 180.0))

time: 57.1 us -> 57.1 us (level)
  no operation moved by 1% of the time
where the time goes in v6:
time: 57.1 us; the launch traced here: 57 us
  Pallas kernels  55.4 us (97%)
  local copies, waits for them, and re-layouts  1.57 us (3%)
    pallas_call x1, Pallas kernels, per_device(): pl.pallas_call(kernel, out_shape=jax.ShapeDtypeStruct(shape, F32), in_spe...  55.4 us
    unnamed x1, local copies, waits for them, and re-layouts  1.57 us

profile of v6, /device:TPU:32, one launch (start us, length us, event | category | flops | bytes accessed | tf_op | source)
XLA Modules:
  0.0 57.0 jit_solution(4411283557040850587)
XLA Ops:
  0.0 55.4 %covariance.1 = f32[2,2,4,2048]{3,2,1,0:T(4,128)} custom-call(f32[2,2,4,2048]{3,2,1,0:T(4,128)} %inc_hbm.1, f32[2,2,4,2048]{3,2,1,0:T(4,128)} %dev_hbm.1, f32[2,4,2048]{2,1,0:T(4,128)} %dx_hbm.1, f32[2,4,2048]{2,1,0:T(4,128)} %dy_hbm.1, f32[2,4,2048]{2,1,0:T(4,128)} %dz_hbm.1, s32[2,4,2048]{2,1,0:T(4,128)} %sea_hbm.1), custom_call_target="tpu_custom_call" | custom-call | tf_op jit(solution)/shard_map/covariance/pallas_call | solution.py:551
  55.4 1.6 %copy.8 = f32[2,2,4,2048]{3,2,1,0:T(4,128)} copy(f32[2,2,4,2048]{3,2,1,0:T(4,128)} %covariance.1) | data formatting | bytes 262144

commit v7 on v6

--- a/solution.py
+++ b/solution.py
@@ -154,7 +154,7 @@
             send(z_send.at[(zh + t) % 2, j], z_recv.at[lev], TO_COLUMNS, at(y, zf, core, j, (zh + t) % 2))
     part = (zl % 2) * 2 + core
     lines_core = zl // 2
-    for c_send, c_recv, phase in ((cy_send, cy_recv, COUPLE_Y), (cx_send, cx_recv, COUPLE_X)):
+    for c_send, c_recv, phase in ((cy_send, cy_recv, COUPLE_Y),):
         for l in range(2):
             for b in (1, 0):
                 zt = 3 * l if b else 1 + l
@@ -182,6 +182,17 @@
                 put(9 + k, down)
 
     wait(z_recv, recv_sem.at[TO_COLUMNS])
+    for c_send, c_recv, phase in ((cx_send, cx_recv, COUPLE_X),):
+        for l in range(2):
+            for b in (1, 0):
+                zt = 3 * l if b else 1 + l
+                target = at(y, zt, lines_core, x, (zh + b) % 2)
+                src, dst = c_send.at[l], c_recv.at[pl.ds(pl.multiple_of(part * 64, 64), 64)]
+                if b == 0:
+                    send_or_keep(src, dst, phase, target, (zl == zt) & (core == lines_core))
+                else:
+                    send(src, dst, phase, target)
+
     upper = lower = jnp.ones((16, 128), F32)
     for k in range(8):
         c_up = z_recv[(k + 1) // 2, 1, (k + 1) % 2]

time: 57.1 us -> 56.8 us (level)
  no operation moved by 1% of the time
where the time goes in v7:
time: 56.8 us; the launch traced here: 56.7 us
  Pallas kernels  55.1 us (97%)
  local copies, waits for them, and re-layouts  1.57 us (3%)
    pallas_call x1, Pallas kernels, per_device(): pl.pallas_call(kernel, out_shape=jax.ShapeDtypeStruct(shape, F32), in_spe...  55.1 us
    unnamed x1, local copies, waits for them, and re-layouts  1.57 us

profile of v7, /device:TPU:32, one launch (start us, length us, event | category | flops | bytes accessed | tf_op | source)
XLA Modules:
  0.0 56.7 jit_solution(5315278216627227962)
XLA Ops:
  0.0 55.1 %covariance.1 = f32[2,2,4,2048]{3,2,1,0:T(4,128)} custom-call(f32[2,2,4,2048]{3,2,1,0:T(4,128)} %inc_hbm.1, f32[2,2,4,2048]{3,2,1,0:T(4,128)} %dev_hbm.1, f32[2,4,2048]{2,1,0:T(4,128)} %dx_hbm.1, f32[2,4,2048]{2,1,0:T(4,128)} %dy_hbm.1, f32[2,4,2048]{2,1,0:T(4,128)} %dz_hbm.1, s32[2,4,2048]{2,1,0:T(4,128)} %sea_hbm.1), custom_call_target="tpu_custom_call" | custom-call | tf_op jit(solution)/shard_map/covariance/pallas_call | solution.py:562
  55.1 1.6 %copy.8 = f32[2,2,4,2048]{3,2,1,0:T(4,128)} copy(f32[2,2,4,2048]{3,2,1,0:T(4,128)} %covariance.1) | data formatting | bytes 262144
